TPU v7x, 512 devices: a whole 4x4x16 slice. The times are simulated.
512 devices in a mesh: space: 128 (over x, y_hi, z), tm: 4 (over y_lo, core).
Axes of the slice: x: 4, y: 4 (y_hi: 2, y_lo: 2; y = y_hi * 2 + y_lo), z: 16, core: 2. Of those that a mesh axis runs over, the one named last changes fastest.
Arguments:
- source_field: float32 [2, 4, 3, 1048576], P(None, None, None, ('tm', 'space')), may hold values from -6 to 6
- initial_guess: float32 [2, 4, 3, 1048576], P(None, None, None, ('tm', 'space')), may hold values from -1.8 to 1.8
- gauge_links: bfloat16 [4, 2, 3, 3, 1048576], P(None, None, None, None, ('tm', 'space')), may hold values from -0.8984375 to 0.8984375
- clover: bfloat16 [2, 2, 6, 6, 1048576], P(None, None, None, None, ('tm', 'space')), may hold values from -1.5 to 8.5
- boundary_signs: int32 [65536], P('space'), may hold values from 0 to 1
- null_vectors: bfloat16 [24, 2, 4, 3, 1048576], P(None, None, None, None, ('tm', 'space')), may hold values from -0.29882812 to 0.29882812
- coarse_ops: bfloat16 [9, 2, 24, 98304], P(None, None, None, ('tm', 'space')), may hold values from -0.41992188 to 0.41992188
Outputs:
- smoothed: float32 [2, 4, 3, 1048576], P(None, None, None, ('tm', 'space'))
- coarse_out: float32 [2, 24, 4096], P(None, None, ('tm', 'space'))
All inputs are finite; a program needn't handle non-finite values.
Results may differ from a plain program's by a relative error of at most 0.0029.
Values sent between devices are 32-bit elements; how exact they have to be, the bound alone decides.
A program may use at most 128 MiB of HBM per device.

v0:
```python
import jax
import jax.numpy as jnp
from jax import lax
from jax.experimental import pallas as pl
from jax.experimental.pallas import tpu as pltpu
from jax.sharding import PartitionSpec as P

F32 = jnp.float32
BF16 = jnp.bfloat16
NV = 24
STRIDES = (32, 8, 1)
SPIN = (
    ((3, "-i"), (2, "-i")),
    ((3, "-1"), (2, "+1")),
    ((2, "-i"), (3, "+i")),
    ((2, "+1"), (3, "+1")),
)
CONJ = {"+1": "+1", "-1": "-1", "+i": "-i", "-i": "+i"}
NEG = {"+1": "-1", "-1": "+1", "+i": "-i", "-i": "+i"}
PAD = 8


def add_phase(acc, x, phase):
    if phase == "+1":
        return acc[0] + x[0], acc[1] + x[1]
    if phase == "-1":
        return acc[0] - x[0], acc[1] - x[1]
    if phase == "+i":
        return acc[0] - x[1], acc[1] + x[0]
    return acc[0] + x[1], acc[1] - x[0]


def lane_roll(x, shift):
    shift = shift % 128
    return x if shift == 0 else pltpu.roll(x, shift, 1)


def row_roll(x, shift):
    shift = shift % 8
    return x if shift == 0 else pltpu.roll(x, shift, 0)


def spinor_rows(p, s, c, v):
    return pl.ds(((p * 3 + c) * 16 + 8 * v) * 4 + s, 8, stride=4)


def mul_add(acc, a, b, conj):
    if conj:
        re, im = a[0] * b[0] + a[1] * b[1], a[0] * b[1] - a[1] * b[0]
    else:
        re, im = a[0] * b[0] - a[1] * b[1], a[0] * b[1] + a[1] * b[0]
    return (re, im) if acc is None else (acc[0] + re, acc[1] + im)


def kernel(
    n_space, n_tm,
    src_hbm, guess_hbm, gauge_hbm, clover_hbm, sign_hbm, null_hbm, ops_hbm,
    smooth_hbm, coarse_ref,
    src, gauge, clover, sign, null, ops,
    vb, rl, lf, cf, nf, of, s8, hb, acc_ref, ez,
    sx, st, rx, rt, wsum, sw, rw, gmat,
    in_sem, out_sem, send_sem, recv_sem,
):
    space = lax.axis_index("space")
    tm = lax.axis_index("tm")
    strides = STRIDES

    def ahead(d):
        if d == 3:
            return {"tm": lax.rem(tm + 1, n_tm)}
        return {"space": lax.rem(space + strides[d], n_space)}

    def behind(d):
        if d == 3:
            return {"tm": lax.rem(tm + n_tm - 1, n_tm)}
        return {"space": lax.rem(space + n_space - strides[d], n_space)}

    loads = [
        pltpu.make_async_copy(guess_hbm, vb.at[0], in_sem.at[0]),
        pltpu.make_async_copy(gauge_hbm, gauge, in_sem.at[1]),
        pltpu.make_async_copy(sign_hbm, sign, in_sem.at[2]),
        pltpu.make_async_copy(clover_hbm, clover, in_sem.at[3]),
        pltpu.make_async_copy(src_hbm, src, in_sem.at[4]),
        pltpu.make_async_copy(null_hbm, null, in_sem.at[5]),
        pltpu.make_async_copy(ops_hbm, ops, in_sem.at[6]),
    ]
    barrier = pltpu.get_barrier_semaphore()
    for d in range(4):
        for target in (ahead(d), behind(d)):
            pl.semaphore_signal(
                barrier, inc=1, device_id=target, device_id_type=pl.DeviceIdType.MESH
            )
    for load in loads:
        load.start()

    lane = lax.broadcasted_iota(jnp.int32, (8, 128), 1)
    row = lax.broadcasted_iota(jnp.int32, (8, 128), 0)
    lx = lane % 8
    ly = lane // 8 % 8
    low_half = lane < 64

    loads[1].wait()
    loads[2].wait()

    def widen_links(i, carry):
        rows = pl.ds(pl.multiple_of(i * 128, 128), 128)
        lf[rows, :] = gauge[rows, :].astype(F32)
        return carry

    lax.fori_loop(0, 9, widen_links, 0)
    sign_rows = (2 * sign[...] - 1).astype(F32)
    sign_rows = jnp.where(tm == n_tm - 1, sign_rows, jnp.ones_like(sign_rows))
    s8[pl.ds(0, 4, stride=2), :] = sign_rows
    s8[pl.ds(1, 4, stride=2), :] = sign_rows
    factor = s8[...]
    for rc in range(9):
        rows = pl.ds((27 + rc) * 32 + 24, 8)
        lf[rows, :] = lf[rows, :] * factor

    ez[...] = jnp.zeros_like(ez)
    hb[:, 0:PAD, :] = jnp.zeros((8, PAD, 128), F32)
    hb[:, PAD + 192 : PAD + 200, :] = jnp.zeros((8, 8, 128), F32)
    rt[:, :, 0:PAD, :] = jnp.zeros((3, 2, PAD, 128), F32)
    rt[:, :, PAD + 48 : PAD + 56, :] = jnp.zeros((3, 2, 8, 128), F32)

    def link(d, r, c, v):
        base = ((d * 9 + r * 3 + c) * 16 + 8 * v) * 2
        return lf[pl.ds(base, 8, stride=2), :], lf[pl.ds(base + 1, 8, stride=2), :]

    loads[0].wait()
    pl.semaphore_wait(barrier, 8)

    def exchange(i, d, forward):
        slot = 2 * d + (0 if forward else 1)
        if d == 3:
            source = st.at[i, slot - 6]
            target = rt.at[i, slot - 6, pl.ds(PAD, 48)]
        else:
            source = sx.at[i, slot]
            target = rx.at[i, slot]
        return pltpu.make_async_remote_copy(
            src_ref=source,
            dst_ref=target,
            send_sem=send_sem.at[i, slot],
            recv_sem=recv_sem.at[i, slot],
            device_id=behind(d) if forward else ahead(d),
            device_id_type=pl.DeviceIdType.MESH,
        )

    def prepare(i, d):
        width = 1 if d == 0 else 8
        which = lx if d == 0 else ly
        faces = {True: [], False: []}
        for v in range(2):
            spin = {}
            for p in range(2):
                for s in range(4):
                    for c in range(3):
                        spin[p, s, c] = vb[i, spinor_rows(p, s, c, v), :]
            half = {True: {}, False: {}}
            for a in range(2):
                source, phase = SPIN[d][a]
                for c in range(3):
                    up = spin[0, a, c], spin[1, a, c]
                    low = spin[0, source, c], spin[1, source, c]
                    half[True][a, c] = add_phase(up, low, NEG[phase])
                    half[False][a, c] = add_phase(up, low, phase)
            carried = {}
            for r in range(3):
                us = [link(d, c, r, v) for c in range(3)]
                for a in range(2):
                    total = None
                    for c in range(3):
                        total = mul_add(total, us[c], half[False][a, c], True)
                    carried[a, r] = total
            half[False] = carried
            for forward in (True, False):
                slot = 2 * d + (0 if forward else 1)
                for a in range(2):
                    for c in range(3):
                        for p in range(2):
                            j = (a * 3 + c) * 2 + p
                            value = half[forward][a, c][p]
                            hb[slot, pl.ds(PAD + j * 16 + 8 * v, 8), :] = value
                            faces[forward].append(value)
        for forward in (True, False):
            slot = 2 * d + (0 if forward else 1)
            values = faces[forward]
            if d < 2:
                for k in range(3):
                    packed = None
                    for m in range(8):
                        shift = m if forward else m - 7
                        moved = lane_roll(values[8 * k + m], width * shift)
                        packed = moved if packed is None else jnp.where(which == m, moved, packed)
                    sx[i, slot, pl.ds(8 * k, 8), :] = packed
            elif d == 2:
                take = 0 if forward else 3
                for j in range(6):
                    for v in range(2):
                        here, there = values[12 * v + j], lane_roll(values[12 * v + j + 6], 64)
                        pair = (
                            jnp.where(low_half, here, there)
                            if forward
                            else jnp.where(low_half, there, here)
                        )
                        ez[2, pl.ds(j * 16 + 8 * v, 8), :] = pair
                for k in range(3):
                    sx[i, slot, pl.ds(8 * k, 8), :] = ez[2, pl.ds(32 * k + take, 8, stride=4), :]
            else:
                for j in range(12):
                    st[i, slot - 6, pl.ds(4 * j, 4), :] = (
                        values[j][0:4, :] if forward else values[12 + j][4:8, :]
                    )
            exchange(i, d, forward).start()

    def shifted(i, d, forward, v):
        slot = 2 * d + (0 if forward else 1)
        out = []
        if d == 2 and v == 0:
            place = 3 if forward else 0
            for k in range(3):
                ez[1 - int(forward), pl.ds(32 * k + place, 8, stride=4), :] = rx[
                    i, slot, pl.ds(8 * k, 8), :
                ]
        for j in range(12):
            base = PAD + j * 16
            if d < 2:
                width = 1 if d == 0 else 8
                which = lx if d == 0 else ly
                m = v * 12 + j
                local = hb[slot, pl.ds(base + 8 * v, 8), :]
                packed = rx[i, slot, pl.ds(m // 8 * 8, 8), :]
                if forward:
                    remote = lane_roll(packed, width * (7 - m % 8))
                    out.append(jnp.where(which == 7, remote, lane_roll(local, -width)))
                else:
                    remote = lane_roll(packed, -width * (m % 8))
                    out.append(jnp.where(which == 0, remote, lane_roll(local, width)))
            elif d == 2:
                local = hb[slot, pl.ds(base + 8 * v, 8), :]
                remote = ez[1 - int(forward), pl.ds(j % 6 * 16 + 8 * v, 8), :]
                if j >= 6:
                    remote = lane_roll(remote, 64)
                if forward:
                    edge = jnp.where(row % 4 == 3, remote, row_roll(local, -1))
                    mixed = jnp.where(low_half, edge, local)
                else:
                    edge = jnp.where(row % 4 == 0, remote, row_roll(local, 1))
                    mixed = jnp.where(low_half, local, edge)
                out.append(lane_roll(mixed, 64))
            elif forward:
                if v == 0:
                    out.append(hb[slot, pl.ds(base + 4, 8), :])
                else:
                    local = hb[slot, pl.ds(base + 12, 8), :]
                    remote = rt[i, 0, pl.ds(PAD + 4 * j - 4, 8), :]
                    out.append(jnp.where(row < 4, local, remote))
            elif v == 1:
                out.append(hb[slot, pl.ds(base + 4, 8), :])
            else:
                local = hb[slot, pl.ds(base - 4, 8), :]
                remote = rt[i, 1, pl.ds(PAD + 4 * j, 8), :]
                out.append(jnp.where(row < 4, remote, local))
        return {(a, c): (out[(a * 3 + c) * 2], out[(a * 3 + c) * 2 + 1]) for a in range(2) for c in range(3)}

    def acc_rows(p, s, c, v):
        return pl.ds(((p * 4 + s) * 3 + c) * 16 + 8 * v, 8)

    def hop(i, d, store):
        exchange(i, d, True).wait_recv()
        exchange(i, d, False).wait_recv()
        for v in range(2):
            front = shifted(i, d, True, v)
            back = shifted(i, d, False, v)
            for r in range(3):
                us = [link(d, r, c, v) for c in range(3)]
                for a in range(2):
                    source, phase = SPIN[d][a]
                    w = None
                    for c in range(3):
                        w = mul_add(w, us[c], front[a, c], False)
                    b = back[a, r]
                    upper = acc_ref[acc_rows(0, a, r, v), :], acc_ref[acc_rows(1, a, r, v), :]
                    lower = (
                        acc_ref[acc_rows(0, source, r, v), :],
                        acc_ref[acc_rows(1, source, r, v), :],
                    )
                    upper = upper[0] + (w[0] + b[0]), upper[1] + (w[1] + b[1])
                    lower = add_phase(lower, (b[0] - w[0], b[1] - w[1]), CONJ[phase])
                    store(upper, a, r, v)
                    store(lower, source, r, v)

    def to_acc(value, s, c, v):
        acc_ref[acc_rows(0, s, c, v), :] = value[0]
        acc_ref[acc_rows(1, s, c, v), :] = value[1]

    def clover_term(i):
        for v in range(2):
            for b in range(2):
                x = [
                    tuple(vb[i, spinor_rows(p, 2 * b + n // 3, n % 3, v), :] for p in range(2))
                    for n in range(6)
                ]
                for r in range(6):
                    total = None
                    for n in range(6):
                        base = ((b * 36 + r * 6 + n) * 16 + 8 * v) * 2
                        c = cf[pl.ds(base, 8, stride=2), :], cf[pl.ds(base + 1, 8, stride=2), :]
                        total = mul_add(total, c, x[n], False)
                    s, c = 2 * b + r // 3, r % 3
                    f = tuple(src[spinor_rows(p, s, c, v), :] for p in range(2))
                    to_acc((2.0 * (f[0] - total[0]), 2.0 * (f[1] - total[1])), s, c, v)

    def widen_null(i, carry):
        rows = pl.ds(pl.multiple_of(i * 256, 256), 256)
        nf[rows, :] = null[rows, :].astype(F32)
        return carry

    def sweep(i, carry):
        prepare(i, 1)
        prepare(i, 0)
        prepare(i, 2)
        prepare(i, 3)

        @pl.when(i == 0)
        def _():
            loads[3].wait()
            loads[4].wait()

            def widen_clover(n, inner):
                rows = pl.ds(pl.multiple_of(n * 256, 256), 256)
                cf[rows, :] = clover[rows, :].astype(F32)
                return inner

            lax.fori_loop(0, 9, widen_clover, 0)

        clover_term(i)
        hop(i, 3, to_acc)
        hop(i, 0, to_acc)
        hop(i, 2, to_acc)

        @pl.when(i == 0)
        def _():
            loads[5].wait()

        lax.fori_loop(i * 12, i * 12 + 12, widen_null, 0)

        def finish(value, s, c, v):
            for p in range(2):
                rows = spinor_rows(p, s, c, v)
                vb[i + 1, rows, :] = vb[i, rows, :] + 0.08 * value[p]
                rl[rows, :] = (0.5 * value[p]).astype(BF16).astype(F32)

        hop(i, 1, finish)
        return carry

    lax.fori_loop(0, 3, sweep, 0)
    smooth = pltpu.make_async_copy(vb.at[2], smooth_hbm, out_sem.at[0])
    smooth.start()

    GROUP = 2

    def restrict(g, carry):
        sums = []
        for n in range(GROUP):
            kv = g * GROUP + n
            total = {}
            for az in range(2):
                re, im = None, None
                for c in range(3):
                    for t in range(4):
                        local = (2 * t + az) * 8
                        n_re = nf[pl.ds(pl.multiple_of((kv * 6 + c) * 64 + local, 8), 8), :]
                        n_im = nf[pl.ds(pl.multiple_of((kv * 6 + 3 + c) * 64 + local, 8), 8), :]
                        r_re = rl[pl.ds(c * 64 + local, 8), :]
                        r_im = rl[pl.ds((3 + c) * 64 + local, 8), :]
                        a = n_re * r_re + n_im * r_im
                        b = n_re * r_im - n_im * r_re
                        re = a if re is None else re + a
                        im = b if im is None else im + b
                total[0, az], total[1, az] = re, im
            sums += [total[0, 0], total[0, 1], total[1, 0], total[1, 1]]
        for bit in (1, 2, 4):
            first = row // bit % 2 == 0
            sums = [
                jnp.where(first, x, y) + row_roll(jnp.where(first, y, x), bit)
                for x, y in zip(sums[0::2], sums[1::2])
            ]
        wsum[pl.ds(pl.multiple_of(g * 8, 8), 8), :] = sums[0]
        return carry

    lax.fori_loop(0, NV // GROUP, restrict, 0)

    def split(x):
        high = x.astype(BF16)
        return high, (x - high.astype(F32)).astype(BF16)

    def dot_nt(a, b):
        return lax.dot_general(a, b, (((1,), (1,)), ((), ())), preferred_element_type=F32)

    lane16 = lax.broadcasted_iota(jnp.int32, (16, 128), 1)
    row16 = lax.broadcasted_iota(jnp.int32, (16, 128), 0)
    member = (lane16 // 32 % 2 * 2 + lane16 // 4 % 2 == row16).astype(F32).astype(BF16)
    out_lane = lax.broadcasted_iota(jnp.int32, (96, 512), 1)
    in_row = lax.broadcasted_iota(jnp.int32, (96, 512), 0)
    q = out_lane % 256 // 24
    match = (
        (in_row // 4 == out_lane % 256 % 24)
        & (in_row // 2 % 2 == out_lane // 256)
        & (in_row % 2 == q // 4)
        & (out_lane % 256 < 192)
    )
    gmat[...] = match.astype(F32).astype(BF16)
    high, low = split(wsum[...])
    partial = dot_nt(member, high) + dot_nt(member, low)
    high, low = split(partial)
    spread = jnp.dot(high, gmat[...], preferred_element_type=F32) + jnp.dot(
        low, gmat[...], preferred_element_type=F32
    )
    spread_lane = lax.broadcasted_iota(jnp.int32, (16, 512), 1)
    spread_row = lax.broadcasted_iota(jnp.int32, (16, 512), 0)
    vector = jnp.sum(
        jnp.where(spread_lane % 256 // 24 % 4 == spread_row, spread, 0.0), axis=0, keepdims=True
    )
    sw[0:1, :] = vector[:, 0:256]
    sw[1:2, :] = vector[:, 256:512]

    def exchange_coarse(d, forward):
        slot = 2 * d + (0 if forward else 1)
        return pltpu.make_async_remote_copy(
            src_ref=sw,
            dst_ref=rw.at[slot],
            send_sem=send_sem.at[3, slot],
            recv_sem=recv_sem.at[3, slot],
            device_id=behind(d) if forward else ahead(d),
            device_id_type=pl.DeviceIdType.MESH,
        )

    order = (1, 0, 2, 3)
    for d in order:
        for forward in (True, False):
            exchange_coarse(d, forward).start()

    loads[6].wait()
    for n in range(18):
        of[n] = ops[n].astype(F32)

    lane1 = lax.broadcasted_iota(jnp.int32, (8, 256), 1)
    own = jnp.broadcast_to(sw[0:1, :], (8, 256)), jnp.broadcast_to(sw[1:2, :], (8, 256))

    def apply(total, n, vec):
        w_re, w_im = vec[0][0:1, 0:192], vec[1][0:1, 0:192]
        o_re, o_im = of[2 * n], of[2 * n + 1]
        re = o_re * w_re - o_im * w_im
        im = o_re * w_im + o_im * w_re
        return (re, im) if total is None else (total[0] + re, total[1] + im)

    total = apply(None, 0, own)
    for d in (3, 0, 2, 1):
        for forward in (True, False):
            slot = 2 * d + (0 if forward else 1)
            exchange_coarse(d, forward).wait_recv()
            vec = []
            for p in range(2):
                remote = jnp.broadcast_to(rw[slot, p : p + 1, :], (8, 256))
                if d == 3:
                    vec.append(remote)
                    continue
                step = 1 << d
                near = lane1 // 24 // step % 2 == (0 if forward else 1)
                left = 256 - 24 * step
                right = 24 * step
                if forward:
                    vec.append(jnp.where(near, pltpu.roll(own[p], left, 1), pltpu.roll(remote, right, 1)))
                else:
                    vec.append(jnp.where(near, pltpu.roll(own[p], right, 1), pltpu.roll(remote, left, 1)))
            total = apply(total, 1 + slot, vec)

    segment = (
        lax.broadcasted_iota(jnp.int32, (16, 192), 1) // 24
        == lax.broadcasted_iota(jnp.int32, (16, 192), 0)
    )
    segment = segment.astype(F32).astype(BF16)
    for p in range(2):
        high, low = split(total[p])
        result = dot_nt(segment, high) + dot_nt(segment, low)
        coarse_ref[p] = result[0:8, :]

    smooth.wait()
    for d in range(4):
        for forward in (True, False):
            for i in range(3):
                exchange(i, d, forward).wait_send()
            exchange_coarse(d, forward).wait_send()


def solution(mesh):
    n_space, n_tm = mesh.shape["space"], mesh.shape["tm"]

    def spinor_in(x):
        return x.transpose(0, 2, 1, 3).reshape(6, 4, 16, 128).transpose(0, 2, 1, 3).reshape(384, 128)

    def spinor_out(x):
        return x.reshape(6, 16, 4, 128).transpose(0, 2, 1, 3).reshape(2, 3, 4, 2048).transpose(0, 2, 1, 3)

    def matrix_in(x, count):
        return (
            x.transpose(0, 2, 3, 1, 4)
            .reshape(count, 2, 16, 128)
            .transpose(0, 2, 1, 3)
            .reshape(count * 32, 128)
        )

    def on_device(source_field, initial_guess, gauge_links, clover, boundary_signs, null_vectors, coarse_ops):
        nulls = (
            null_vectors.transpose(0, 1, 3, 2, 4)
            .reshape(144, 4, 16, 128)
            .transpose(0, 2, 1, 3)
            .reshape(9216, 128)
        )
        vmem = pltpu.VMEM
        smoothed, coarse = pl.pallas_call(
            lambda *refs: kernel(n_space, n_tm, *refs),
            out_shape=(
                jax.ShapeDtypeStruct((384, 128), F32),
                jax.ShapeDtypeStruct((2, 8, 24), F32),
            ),
            in_specs=[pl.BlockSpec(memory_space=pl.ANY)] * 7,
            out_specs=(pl.BlockSpec(memory_space=pl.ANY), pl.BlockSpec(memory_space=vmem)),
            scratch_shapes=[
                vmem((384, 128), F32),
                vmem((1152, 128), BF16),
                vmem((2304, 128), BF16),
                vmem((4, 128), jnp.int32),
                vmem((9216, 128), BF16),
                vmem((18, 24, 192), BF16),
                vmem((4, 384, 128), F32),
                vmem((384, 128), F32),
                vmem((1152, 128), F32),
                vmem((2304, 128), F32),
                vmem((9216, 128), F32),
                vmem((18, 24, 192), F32),
                vmem((8, 128), F32),
                vmem((8, 208, 128), F32),
                vmem((384, 128), F32),
                vmem((3, 96, 128), F32),
                vmem((3, 6, 24, 128), F32),
                vmem((3, 2, 48, 128), F32),
                vmem((3, 6, 24, 128), F32),
                vmem((3, 2, 64, 128), F32),
                vmem((96, 128), F32),
                vmem((2, 256), F32),
                vmem((8, 2, 256), F32),
                vmem((96, 512), BF16),
                pltpu.SemaphoreType.DMA((7,)),
                pltpu.SemaphoreType.DMA((1,)),
                pltpu.SemaphoreType.DMA((4, 8)),
                pltpu.SemaphoreType.DMA((4, 8)),
            ],
            compiler_params=pltpu.CompilerParams(
                collective_id=0, has_side_effects=True, vmem_limit_bytes=60 * 1024 * 1024
            ),
        )(
            spinor_in(source_field),
            spinor_in(initial_guess),
            matrix_in(gauge_links, 36),
            matrix_in(clover, 72),
            boundary_signs.reshape(4, 128),
            nulls,
            coarse_ops.reshape(18, 24, 192),
        )
        return spinor_out(smoothed), coarse.transpose(0, 2, 1)

    field = P(None, None, None, ("tm", "space"))
    matrix = P(None, None, None, None, ("tm", "space"))
    return jax.shard_map(
        on_device,
        mesh=mesh,
        in_specs=(field, field, matrix, matrix, P("space"), matrix, field),
        out_specs=(field, P(None, None, ("tm", "space"))),
        check_vma=False,
    )
```

profile of v0, /device:TPU:32, one launch (start us, length us, event | category | flops | bytes accessed | tf_op | source)
XLA Modules:
  0.0 63.2 jit_solution(4450449648852711877)
XLA Ops:
  0.6 59.6 %shard_map.86 = (f32[384,128]{1,0:T(8,128)}, f32[2,8,24]{2,1,0:T(8,128)}) custom-call(f32[384,128]{1,0:T(8,128)} %bitcast.49, f32[384,128]{1,0:T(8,128)} %bitcast.50, bf16[1152,128]{1,0:T(8,128)(2,1)} %bitcast.47, bf16[2304,128]{1,0:T(8,128)(2,1)} %bitcast.46, s32[4,128]{1,0:T(4,128)} %bitcast.53, bf16[9216,128]{1,0:T(8,128)(2,1)} %bitcast.45, ...), custom_call_target="tpu_custom_call" | custom-call | tf_op jit(solution)/shard_map/pallas_call | solution.py:523
  60.3 1.6 %copy.16 = f32[2,4,3,2048]{3,1,2,0:T(4,128)} copy(f32[2,4,3,2048]{3,1,2,0:T(4,128)} %bitcast.51) | data formatting | bytes 393216
  61.9 1.3 %copy.17 = f32[2,24,8]{1,2,0:T(8,128)} copy(f32[2,24,8]{1,2,0:T(8,128)} %bitcast.52) | data formatting | bytes 3072
where the time goes:
time: 63.4 us; the launch traced here: 63.2 us
  Pallas kernels  59.6 us (94%)
  local copies, waits for them, and re-layouts  2.91 us (5%)
  between operations  0.64 us (1%)
    pallas_call x1, Pallas kernels, on_device(): pl.pallas_call(lambda *refs: kernel(n_space, n_tm, *refs), out_shape=(jax...  59.6 us
    unnamed x2, local copies, waits for them, and re-layouts  2.91 us

commit v1 on v0

--- a/solution.py
+++ b/solution.py
@@ -55,11 +55,11 @@
 def kernel(
     n_space, n_tm,
     src_hbm, guess_hbm, gauge_hbm, clover_hbm, sign_hbm, null_hbm, ops_hbm,
-    smooth_hbm, coarse_ref,
+    smooth_ref, coarse_ref,
     src, gauge, clover, sign, null, ops,
     vb, rl, lf, cf, nf, of, s8, hb, acc_ref, ez,
     sx, st, rx, rt, wsum, sw, rw, gmat,
-    in_sem, out_sem, send_sem, recv_sem,
+    in_sem, send_sem, recv_sem,
 ):
     space = lax.axis_index("space")
     tm = lax.axis_index("tm")
@@ -127,9 +127,6 @@
         base = ((d * 9 + r * 3 + c) * 16 + 8 * v) * 2
         return lf[pl.ds(base, 8, stride=2), :], lf[pl.ds(base + 1, 8, stride=2), :]
 
-    loads[0].wait()
-    pl.semaphore_wait(barrier, 8)
-
     def exchange(i, d, forward):
         slot = 2 * d + (0 if forward else 1)
         if d == 3:
@@ -147,7 +144,7 @@
             device_id_type=pl.DeviceIdType.MESH,
         )
 
-    def prepare(i, d):
+    def prepare(i, d, read, keep, pack):
         width = 1 if d == 0 else 8
         which = lx if d == 0 else ly
         faces = {True: [], False: []}
@@ -156,7 +153,7 @@
             for p in range(2):
                 for s in range(4):
                     for c in range(3):
-                        spin[p, s, c] = vb[i, spinor_rows(p, s, c, v), :]
+                        spin[p, s, c] = read(p, s, c, v)
             half = {True: {}, False: {}}
             for a in range(2):
                 source, phase = SPIN[d][a]
@@ -181,8 +178,11 @@
                         for p in range(2):
                             j = (a * 3 + c) * 2 + p
                             value = half[forward][a, c][p]
-                            hb[slot, pl.ds(PAD + j * 16 + 8 * v, 8), :] = value
+                            if keep:
+                                hb[slot, pl.ds(PAD + j * 16 + 8 * v, 8), :] = value
                             faces[forward].append(value)
+        if not pack:
+            return
         for forward in (True, False):
             slot = 2 * d + (0 if forward else 1)
             values = faces[forward]
@@ -212,9 +212,12 @@
                     st[i, slot - 6, pl.ds(4 * j, 4), :] = (
                         values[j][0:4, :] if forward else values[12 + j][4:8, :]
                     )
+
+    def send(i, d):
+        for forward in (True, False):
             exchange(i, d, forward).start()
 
-    def shifted(i, d, forward, v):
+    def shifted(i, d, forward, v, part):
         slot = 2 * d + (0 if forward else 1)
         out = []
         if d == 2 and v == 0:
@@ -231,12 +234,13 @@
                 m = v * 12 + j
                 local = hb[slot, pl.ds(base + 8 * v, 8), :]
                 packed = rx[i, slot, pl.ds(m // 8 * 8, 8), :]
-                if forward:
-                    remote = lane_roll(packed, width * (7 - m % 8))
-                    out.append(jnp.where(which == 7, remote, lane_roll(local, -width)))
-                else:
-                    remote = lane_roll(packed, -width * (m % 8))
-                    out.append(jnp.where(which == 0, remote, lane_roll(local, width)))
+                edge = which == (7 if forward else 0)
+                far = near = 0.0
+                if part != "local":
+                    far = lane_roll(packed, width * (7 - m % 8 if forward else -(m % 8)))
+                if part != "remote":
+                    near = lane_roll(local, -width if forward else width)
+                out.append(jnp.where(edge, far, near))
             elif d == 2:
                 local = hb[slot, pl.ds(base + 8 * v, 8), :]
                 remote = ez[1 - int(forward), pl.ds(j % 6 * 16 + 8 * v, 8), :]
@@ -267,12 +271,13 @@
     def acc_rows(p, s, c, v):
         return pl.ds(((p * 4 + s) * 3 + c) * 16 + 8 * v, 8)
 
-    def hop(i, d, store):
-        exchange(i, d, True).wait_recv()
-        exchange(i, d, False).wait_recv()
+    def hop(i, d, store, part="both"):
+        if part != "local":
+            exchange(i, d, True).wait_recv()
+            exchange(i, d, False).wait_recv()
         for v in range(2):
-            front = shifted(i, d, True, v)
-            back = shifted(i, d, False, v)
+            front = shifted(i, d, True, v, part)
+            back = shifted(i, d, False, v, part)
             for r in range(3):
                 us = [link(d, r, c, v) for c in range(3)]
                 for a in range(2):
@@ -317,47 +322,76 @@
         nf[rows, :] = null[rows, :].astype(F32)
         return carry
 
-    def sweep(i, carry):
-        prepare(i, 1)
-        prepare(i, 0)
-        prepare(i, 2)
-        prepare(i, 3)
-
-        @pl.when(i == 0)
-        def _():
-            loads[3].wait()
-            loads[4].wait()
-
-            def widen_clover(n, inner):
-                rows = pl.ds(pl.multiple_of(n * 256, 256), 256)
-                cf[rows, :] = clover[rows, :].astype(F32)
-                return inner
-
-            lax.fori_loop(0, 9, widen_clover, 0)
-
+    def current(i):
+        return lambda p, s, c, v: vb[i, spinor_rows(p, s, c, v), :]
+
+    def without_y(i):
+        return lambda p, s, c, v: vb[i, spinor_rows(p, s, c, v), :] + 0.08 * acc_ref[acc_rows(p, s, c, v), :]
+
+    def sweep(i, last):
         clover_term(i)
+        hop(i, 1, to_acc, "local")
         hop(i, 3, to_acc)
         hop(i, 0, to_acc)
         hop(i, 2, to_acc)
-
-        @pl.when(i == 0)
-        def _():
-            loads[5].wait()
-
-        lax.fori_loop(i * 12, i * 12 + 12, widen_null, 0)
+        if not last:
+            prepare(i + 1, 1, without_y(i), False, True)
+            send(i + 1, 1)
 
         def finish(value, s, c, v):
             for p in range(2):
                 rows = spinor_rows(p, s, c, v)
-                vb[i + 1, rows, :] = vb[i, rows, :] + 0.08 * value[p]
-                rl[rows, :] = (0.5 * value[p]).astype(BF16).astype(F32)
-
-        hop(i, 1, finish)
+                if last:
+                    rl[rows, :] = (0.5 * value[p]).astype(BF16).astype(F32)
+                else:
+                    vb[i + 1, rows, :] = vb[i, rows, :] + 0.08 * value[p]
+
+        hop(i, 1, finish, "remote")
+        if not last:
+            for d in (2, 0, 3):
+                prepare(i + 1, d, current(i + 1), True, True)
+                send(i + 1, d)
+            prepare(i + 1, 1, current(i + 1), True, False)
+
+    loads[0].wait()
+    for d in (1, 2, 0, 3):
+        prepare(0, d, current(0), True, True)
+    pl.semaphore_wait(barrier, 8)
+    for d in (1, 2, 0, 3):
+        send(0, d)
+
+    loads[3].wait()
+
+    def widen_clover(n, carry):
+        rows = pl.ds(pl.multiple_of(n * 256, 256), 256)
+        cf[rows, :] = clover[rows, :].astype(F32)
         return carry
 
-    lax.fori_loop(0, 3, sweep, 0)
-    smooth = pltpu.make_async_copy(vb.at[2], smooth_hbm, out_sem.at[0])
-    smooth.start()
+    lax.fori_loop(0, 9, widen_clover, 0)
+    loads[5].wait()
+    lax.fori_loop(0, 36, widen_null, 0)
+    loads[6].wait()
+    for n in range(18):
+        of[n] = ops[n].astype(F32)
+    out_lane = lax.broadcasted_iota(jnp.int32, (96, 512), 1)
+    in_row = lax.broadcasted_iota(jnp.int32, (96, 512), 0)
+    q = out_lane % 256 // 24
+    match = (
+        (in_row // 4 == out_lane % 256 % 24)
+        & (in_row // 2 % 2 == out_lane // 256)
+        & (in_row % 2 == q // 4)
+        & (out_lane % 256 < 192)
+    )
+    gmat[...] = match.astype(F32).astype(BF16)
+    loads[4].wait()
+
+    def first_sweeps(i, carry):
+        sweep(i, False)
+        return carry
+
+    lax.fori_loop(0, 2, first_sweeps, 0)
+    smooth_ref[...] = vb[2]
+    sweep(2, True)
 
     GROUP = 2
 
@@ -402,16 +436,6 @@
     lane16 = lax.broadcasted_iota(jnp.int32, (16, 128), 1)
     row16 = lax.broadcasted_iota(jnp.int32, (16, 128), 0)
     member = (lane16 // 32 % 2 * 2 + lane16 // 4 % 2 == row16).astype(F32).astype(BF16)
-    out_lane = lax.broadcasted_iota(jnp.int32, (96, 512), 1)
-    in_row = lax.broadcasted_iota(jnp.int32, (96, 512), 0)
-    q = out_lane % 256 // 24
-    match = (
-        (in_row // 4 == out_lane % 256 % 24)
-        & (in_row // 2 % 2 == out_lane // 256)
-        & (in_row % 2 == q // 4)
-        & (out_lane % 256 < 192)
-    )
-    gmat[...] = match.astype(F32).astype(BF16)
     high, low = split(wsum[...])
     partial = dot_nt(member, high) + dot_nt(member, low)
     high, low = split(partial)
@@ -441,10 +465,6 @@
     for d in order:
         for forward in (True, False):
             exchange_coarse(d, forward).start()
-
-    loads[6].wait()
-    for n in range(18):
-        of[n] = ops[n].astype(F32)
 
     lane1 = lax.broadcasted_iota(jnp.int32, (8, 256), 1)
     own = jnp.broadcast_to(sw[0:1, :], (8, 256)), jnp.broadcast_to(sw[1:2, :], (8, 256))
@@ -487,12 +507,22 @@
         result = dot_nt(segment, high) + dot_nt(segment, low)
         coarse_ref[p] = result[0:8, :]
 
-    smooth.wait()
     for d in range(4):
         for forward in (True, False):
             for i in range(3):
                 exchange(i, d, forward).wait_send()
             exchange_coarse(d, forward).wait_send()
+
+
+def hand_on(smooth_in, coarse_in, smooth_out, coarse_out, sem):
+    copies = [
+        pltpu.make_async_copy(smooth_in, smooth_out, sem.at[0]),
+        pltpu.make_async_copy(coarse_in, coarse_out, sem.at[1]),
+    ]
+    for copy in copies:
+        copy.start()
+    for copy in copies:
+        copy.wait()
 
 
 def solution(mesh):
@@ -527,7 +557,7 @@
                 jax.ShapeDtypeStruct((2, 8, 24), F32),
             ),
             in_specs=[pl.BlockSpec(memory_space=pl.ANY)] * 7,
-            out_specs=(pl.BlockSpec(memory_space=pl.ANY), pl.BlockSpec(memory_space=vmem)),
+            out_specs=(pl.BlockSpec(memory_space=vmem), pl.BlockSpec(memory_space=vmem)),
             scratch_shapes=[
                 vmem((384, 128), F32),
                 vmem((1152, 128), BF16),
@@ -554,7 +584,6 @@
                 vmem((8, 2, 256), F32),
                 vmem((96, 512), BF16),
                 pltpu.SemaphoreType.DMA((7,)),
-                pltpu.SemaphoreType.DMA((1,)),
                 pltpu.SemaphoreType.DMA((4, 8)),
                 pltpu.SemaphoreType.DMA((4, 8)),
             ],
@@ -570,6 +599,16 @@
             nulls,
             coarse_ops.reshape(18, 24, 192),
         )
+        smoothed, coarse = pl.pallas_call(
+            hand_on,
+            out_shape=(
+                jax.ShapeDtypeStruct((384, 128), F32),
+                jax.ShapeDtypeStruct((2, 8, 24), F32),
+            ),
+            in_specs=[pl.BlockSpec(memory_space=vmem)] * 2,
+            out_specs=[pl.BlockSpec(memory_space=pl.ANY)] * 2,
+            scratch_shapes=[pltpu.SemaphoreType.DMA((2,))],
+        )(smoothed, coarse)
         return spinor_out(smoothed), coarse.transpose(0, 2, 1)
 
     field = P(None, None, None, ("tm", "space"))

time: 63.4 us -> 57.2 us (0.902)
  the two profiles are of different devices: /device:TPU:32 before, /device:TPU:8 now
where the time goes in v1:
time: 57.2 us; the launch traced here: 57 us
  Pallas kernels  56.4 us (99%)
  between operations  0.64 us (1%)
    pallas_call x1, Pallas kernels, on_device(): pl.pallas_call(lambda *refs: kernel(n_space, n_tm, *refs), out_shape=(jax...  54.8 us
    pallas_call x1, Pallas kernels, on_device(): pl.pallas_call(hand_on, out_shape=(jax.ShapeDtypeStruct((384, 128), F32),...  1.62 us

profile of v1, /device:TPU:8, one launch (start us, length us, event | category | flops | bytes accessed | tf_op | source)
XLA Modules:
  0.0 57.0 jit_solution(18415944874281371628)
XLA Ops:
  0.6 54.8 %shard_map.86 = (f32[384,128]{1,0:T(8,128)}, f32[2,8,24]{2,1,0:T(8,128)}) custom-call(f32[384,128]{1,0:T(8,128)} %bitcast.49, f32[384,128]{1,0:T(8,128)} %bitcast.50, bf16[1152,128]{1,0:T(8,128)(2,1)} %bitcast.47, bf16[2304,128]{1,0:T(8,128)(2,1)} %bitcast.46, s32[4,128]{1,0:T(4,128)} %bitcast.51, bf16[9216,128]{1,0:T(8,128)(2,1)} %bitcast.45, ...), custom_call_target="tpu_custom_call" | custom-call | tf_op jit(solution)/shard_map/pallas_call | solution.py:553
  55.4 1.6 %shard_map.87 = (f32[384,128]{1,0:T(8,128)}, f32[2,8,24]{2,1,0:T(8,128)}) custom-call(f32[384,128]{1,0:T(8,128)} %get-tuple-element.6.smooth_in, f32[2,8,24]{2,1,0:T(8,128)} %get-tuple-element.7.coarse_in), custom_call_target="tpu_custom_call" | custom-call | tf_op jit(solution)/shard_map/pallas_call | solution.py:602

commit v2 on v1

--- a/solution.py
+++ b/solution.py
@@ -58,7 +58,7 @@
     smooth_ref, coarse_ref,
     src, gauge, clover, sign, null, ops,
     vb, rl, lf, cf, nf, of, s8, hb, acc_ref, ez,
-    sx, st, rx, rt, wsum, sw, rw, gmat,
+    sx, st, rx, rt, wsum, inner, nb, rb, sw, rw, gmat,
     in_sem, send_sem, recv_sem,
 ):
     space = lax.axis_index("space")
@@ -85,7 +85,7 @@
         pltpu.make_async_copy(ops_hbm, ops, in_sem.at[6]),
     ]
     barrier = pltpu.get_barrier_semaphore()
-    for d in range(4):
+    for d in (1, 2, 0, 3):
         for target in (ahead(d), behind(d)):
             pl.semaphore_signal(
                 barrier, inc=1, device_id=target, device_id_type=pl.DeviceIdType.MESH
@@ -328,6 +328,85 @@
     def without_y(i):
         return lambda p, s, c, v: vb[i, spinor_rows(p, s, c, v), :] + 0.08 * acc_ref[acc_rows(p, s, c, v), :]
 
+    GROUP = 2
+
+    def restrict(null_ref, res_ref, steps, part, unroll):
+        def group(g, carry):
+            sums = []
+            for n in range(GROUP):
+                kv = g * GROUP + n
+                total = {}
+                for az in range(2):
+                    re, im = None, None
+                    for c in range(3):
+                        for t in range(steps):
+                            at = c * 16 * steps + (2 * t + az) * 8
+                            half = 48 * steps
+                            base = kv * 96 * steps + at
+                            n_re = null_ref[pl.ds(pl.multiple_of(base, 8), 8), :]
+                            n_im = null_ref[pl.ds(pl.multiple_of(base + half, 8), 8), :]
+                            r_re = res_ref[pl.ds(at, 8), :]
+                            r_im = res_ref[pl.ds(half + at, 8), :]
+                            x = n_re * r_re + n_im * r_im
+                            y = n_re * r_im - n_im * r_re
+                            re = x if re is None else re + x
+                            im = y if im is None else im + y
+                    total[0, az], total[1, az] = re, im
+                sums += [total[0, 0], total[0, 1], total[1, 0], total[1, 1]]
+            for bit in (1, 2, 4):
+                first = row // bit % 2 == 0
+                sums = [
+                    jnp.where(first, x, y) + row_roll(jnp.where(first, y, x), bit)
+                    for x, y in zip(sums[0::2], sums[1::2])
+                ]
+            wsum[part, pl.ds(pl.multiple_of(g * 8, 8), 8), :] = sums[0]
+            return carry
+
+        lax.fori_loop(0, NV // GROUP, group, 0, unroll=unroll)
+
+    side = [((lane // 8 - 2 * t) % 8 == 0) | ((lane // 8 - 2 * t) % 8 == 7) for t in range(4)]
+
+    def fold(parts):
+        out = parts[0]
+        for t in range(1, 4):
+            out = jnp.where(side[t], lane_roll(parts[t], 16 * t), out)
+        return out
+
+    def fold_null(n, carry):
+        for az in range(2):
+            parts = [nf[pl.ds(pl.multiple_of(n * 64 + (2 * t + az) * 8, 8), 8), :] for t in range(4)]
+            nb[pl.ds(pl.multiple_of(n * 16 + az * 8, 8), 8), :] = fold(parts)
+        return carry
+
+    def split(x):
+        high = x.astype(BF16)
+        return jnp.concatenate([high, (x - high.astype(F32)).astype(BF16)], axis=1)
+
+    def dot_nt(a, b):
+        return lax.dot_general(a, b, (((1,), (1,)), ((), ())), preferred_element_type=F32)
+
+    def sums_of(part, member):
+        return dot_nt(member, split(wsum[part]))
+
+    lane16 = lax.broadcasted_iota(jnp.int32, (16, 256), 1) % 128
+    row16 = lax.broadcasted_iota(jnp.int32, (16, 256), 0)
+    inner_member = (lane16 // 32 % 2 * 2 + lane16 // 4 % 2 == row16).astype(F32).astype(BF16)
+    outer_member = (lane16 // 8 % 2 * 2 + lane16 // 4 % 2 == row16).astype(F32).astype(BF16)
+    spread_lane = lax.broadcasted_iota(jnp.int32, (16, 512), 1)
+    spread_row = lax.broadcasted_iota(jnp.int32, (16, 512), 0)
+    spread_mask = spread_lane % 256 // 24 % 4 == spread_row
+
+    def inner_layers():
+        for p in range(2):
+            for s in range(4):
+                for c in range(3):
+                    for v in range(2):
+                        value = 0.5 * acc_ref[acc_rows(p, s, c, v), :]
+                        value = jnp.where((ly == 0) | (ly == 7), 0.0, value)
+                        rl[spinor_rows(p, s, c, v), :] = value.astype(BF16).astype(F32)
+        restrict(nf, rl, 4, 0, 1)
+        inner[...] = sums_of(0, inner_member)
+
     def sweep(i, last):
         clover_term(i)
         hop(i, 1, to_acc, "local")
@@ -337,6 +416,8 @@
         if not last:
             prepare(i + 1, 1, without_y(i), False, True)
             send(i + 1, 1)
+        else:
+            inner_layers()
 
         def finish(value, s, c, v):
             for p in range(2):
@@ -373,16 +454,19 @@
     loads[6].wait()
     for n in range(18):
         of[n] = ops[n].astype(F32)
-    out_lane = lax.broadcasted_iota(jnp.int32, (96, 512), 1)
-    in_row = lax.broadcasted_iota(jnp.int32, (96, 512), 0)
+    out_lane = lax.broadcasted_iota(jnp.int32, (256, 512), 1)
+    in_row = lax.broadcasted_iota(jnp.int32, (256, 512), 0) % 128
     q = out_lane % 256 // 24
     match = (
         (in_row // 4 == out_lane % 256 % 24)
         & (in_row // 2 % 2 == out_lane // 256)
         & (in_row % 2 == q // 4)
         & (out_lane % 256 < 192)
+        & (in_row < 96)
     )
     gmat[...] = match.astype(F32).astype(BF16)
+    wsum[:, 96:128, :] = jnp.zeros((2, 32, 128), F32)
+    lax.fori_loop(0, 144, fold_null, 0, unroll=16)
     loads[4].wait()
 
     def first_sweeps(i, carry):
@@ -393,60 +477,16 @@
     smooth_ref[...] = vb[2]
     sweep(2, True)
 
-    GROUP = 2
-
-    def restrict(g, carry):
-        sums = []
-        for n in range(GROUP):
-            kv = g * GROUP + n
-            total = {}
-            for az in range(2):
-                re, im = None, None
-                for c in range(3):
-                    for t in range(4):
-                        local = (2 * t + az) * 8
-                        n_re = nf[pl.ds(pl.multiple_of((kv * 6 + c) * 64 + local, 8), 8), :]
-                        n_im = nf[pl.ds(pl.multiple_of((kv * 6 + 3 + c) * 64 + local, 8), 8), :]
-                        r_re = rl[pl.ds(c * 64 + local, 8), :]
-                        r_im = rl[pl.ds((3 + c) * 64 + local, 8), :]
-                        a = n_re * r_re + n_im * r_im
-                        b = n_re * r_im - n_im * r_re
-                        re = a if re is None else re + a
-                        im = b if im is None else im + b
-                total[0, az], total[1, az] = re, im
-            sums += [total[0, 0], total[0, 1], total[1, 0], total[1, 1]]
-        for bit in (1, 2, 4):
-            first = row // bit % 2 == 0
-            sums = [
-                jnp.where(first, x, y) + row_roll(jnp.where(first, y, x), bit)
-                for x, y in zip(sums[0::2], sums[1::2])
-            ]
-        wsum[pl.ds(pl.multiple_of(g * 8, 8), 8), :] = sums[0]
-        return carry
-
-    lax.fori_loop(0, NV // GROUP, restrict, 0)
-
-    def split(x):
-        high = x.astype(BF16)
-        return high, (x - high.astype(F32)).astype(BF16)
-
-    def dot_nt(a, b):
-        return lax.dot_general(a, b, (((1,), (1,)), ((), ())), preferred_element_type=F32)
-
-    lane16 = lax.broadcasted_iota(jnp.int32, (16, 128), 1)
-    row16 = lax.broadcasted_iota(jnp.int32, (16, 128), 0)
-    member = (lane16 // 32 % 2 * 2 + lane16 // 4 % 2 == row16).astype(F32).astype(BF16)
-    high, low = split(wsum[...])
-    partial = dot_nt(member, high) + dot_nt(member, low)
-    high, low = split(partial)
-    spread = jnp.dot(high, gmat[...], preferred_element_type=F32) + jnp.dot(
-        low, gmat[...], preferred_element_type=F32
-    )
-    spread_lane = lax.broadcasted_iota(jnp.int32, (16, 512), 1)
-    spread_row = lax.broadcasted_iota(jnp.int32, (16, 512), 0)
-    vector = jnp.sum(
-        jnp.where(spread_lane % 256 // 24 % 4 == spread_row, spread, 0.0), axis=0, keepdims=True
-    )
+    for n in range(6):
+        for az in range(2):
+            rb[pl.ds((n * 2 + az) * 8, 8), :] = fold(
+                [rl[pl.ds(n * 64 + (2 * t + az) * 8, 8), :] for t in range(4)]
+            )
+    restrict(nb, rb, 1, 1, 12)
+    partial = sums_of(1, outer_member) + inner[...]
+
+    spread = jnp.dot(split(partial), gmat[...], preferred_element_type=F32)
+    vector = jnp.sum(jnp.where(spread_mask, spread, 0.0), axis=0, keepdims=True)
     sw[0:1, :] = vector[:, 0:256]
     sw[1:2, :] = vector[:, 256:512]
 
@@ -497,13 +537,11 @@
                     vec.append(jnp.where(near, pltpu.roll(own[p], right, 1), pltpu.roll(remote, left, 1)))
             total = apply(total, 1 + slot, vec)
 
-    segment = (
-        lax.broadcasted_iota(jnp.int32, (16, 192), 1) // 24
-        == lax.broadcasted_iota(jnp.int32, (16, 192), 0)
-    )
-    segment = segment.astype(F32).astype(BF16)
+    seg_lane = lax.broadcasted_iota(jnp.int32, (16, 192), 1)
+    segment = (seg_lane // 24 == lax.broadcasted_iota(jnp.int32, (16, 192), 0)).astype(F32).astype(BF16)
     for p in range(2):
-        high, low = split(total[p])
+        high = total[p].astype(BF16)
+        low = (total[p] - high.astype(F32)).astype(BF16)
         result = dot_nt(segment, high) + dot_nt(segment, low)
         coarse_ref[p] = result[0:8, :]
 
@@ -579,10 +617,13 @@
                 vmem((3, 2, 48, 128), F32),
                 vmem((3, 6, 24, 128), F32),
                 vmem((3, 2, 64, 128), F32),
+                vmem((2, 128, 128), F32),
+                vmem((16, 128), F32),
+                vmem((2304, 128), F32),
                 vmem((96, 128), F32),
                 vmem((2, 256), F32),
                 vmem((8, 2, 256), F32),
-                vmem((96, 512), BF16),
+                vmem((256, 512), BF16),
                 pltpu.SemaphoreType.DMA((7,)),
                 pltpu.SemaphoreType.DMA((4, 8)),
                 pltpu.SemaphoreType.DMA((4, 8)),

time: 57.2 us -> 56.4 us (0.986)
  Pallas kernels: 56.4 us -> 55.7 us
    pallas_call x1, Pallas kernels: 54.8 us -> 54 us  [on_device(): pl.pallas_call(lambda *refs: kernel(n_space, n_tm, *refs), out_shape=(jax...]
where the time goes in v2:
time: 56.4 us; the launch traced here: 56.3 us
  Pallas kernels  55.7 us (99%)
  between operations  0.64 us (1%)
    pallas_call x1, Pallas kernels, on_device(): pl.pallas_call(lambda *refs: kernel(n_space, n_tm, *refs), out_shape=(jax...  54 us
    pallas_call x1, Pallas kernels, on_device(): pl.pallas_call(hand_on, out_shape=(jax.ShapeDtypeStruct((384, 128), F32),...  1.62 us

profile of v2, /device:TPU:8, one launch (start us, length us, event | category | flops | bytes accessed | tf_op | source)
XLA Modules:
  0.0 56.3 jit_solution(4580558619534104500)
XLA Ops:
  0.6 54.0 %shard_map.86 = (f32[384,128]{1,0:T(8,128)}, f32[2,8,24]{2,1,0:T(8,128)}) custom-call(f32[384,128]{1,0:T(8,128)} %bitcast.49, f32[384,128]{1,0:T(8,128)} %bitcast.50, bf16[1152,128]{1,0:T(8,128)(2,1)} %bitcast.47, bf16[2304,128]{1,0:T(8,128)(2,1)} %bitcast.46, s32[4,128]{1,0:T(4,128)} %bitcast.51, bf16[9216,128]{1,0:T(8,128)(2,1)} %bitcast.45, ...), custom_call_target="tpu_custom_call" | custom-call | tf_op jit(solution)/shard_map/pallas_call | solution.py:591
  54.7 1.6 %shard_map.87 = (f32[384,128]{1,0:T(8,128)}, f32[2,8,24]{2,1,0:T(8,128)}) custom-call(f32[384,128]{1,0:T(8,128)} %get-tuple-element.6.smooth_in, f32[2,8,24]{2,1,0:T(8,128)} %get-tuple-element.7.coarse_in), custom_call_target="tpu_custom_call" | custom-call | tf_op jit(solution)/shard_map/pallas_call | solution.py:643

commit v3 on v2

--- a/solution.py
+++ b/solution.py
@@ -144,7 +144,7 @@
             device_id_type=pl.DeviceIdType.MESH,
         )
 
-    def prepare(i, d, read, keep, pack):
+    def prepare(i, d, read, keep, pack, start=False, ways=(True, False)):
         width = 1 if d == 0 else 8
         which = lx if d == 0 else ly
         faces = {True: [], False: []}
@@ -163,7 +163,7 @@
                     half[True][a, c] = add_phase(up, low, NEG[phase])
                     half[False][a, c] = add_phase(up, low, phase)
             carried = {}
-            for r in range(3):
+            for r in range(3 if False in ways else 0):
                 us = [link(d, c, r, v) for c in range(3)]
                 for a in range(2):
                     total = None
@@ -171,7 +171,7 @@
                         total = mul_add(total, us[c], half[False][a, c], True)
                     carried[a, r] = total
             half[False] = carried
-            for forward in (True, False):
+            for forward in ways:
                 slot = 2 * d + (0 if forward else 1)
                 for a in range(2):
                     for c in range(3):
@@ -183,7 +183,7 @@
                             faces[forward].append(value)
         if not pack:
             return
-        for forward in (True, False):
+        for forward in ways:
             slot = 2 * d + (0 if forward else 1)
             values = faces[forward]
             if d < 2:
@@ -212,6 +212,8 @@
                     st[i, slot - 6, pl.ds(4 * j, 4), :] = (
                         values[j][0:4, :] if forward else values[12 + j][4:8, :]
                     )
+            if start:
+                exchange(i, d, forward).start()
 
     def send(i, d):
         for forward in (True, False):
@@ -414,8 +416,8 @@
         hop(i, 0, to_acc)
         hop(i, 2, to_acc)
         if not last:
-            prepare(i + 1, 1, without_y(i), False, True)
-            send(i + 1, 1)
+            for way in (True, False):
+                prepare(i + 1, 1, without_y(i), False, True, True, (way,))
         else:
             inner_layers()
 
@@ -430,8 +432,8 @@
         hop(i, 1, finish, "remote")
         if not last:
             for d in (2, 0, 3):
-                prepare(i + 1, d, current(i + 1), True, True)
-                send(i + 1, d)
+                for way in (False, True):
+                    prepare(i + 1, d, current(i + 1), True, True, True, (way,))
             prepare(i + 1, 1, current(i + 1), True, False)
 
     loads[0].wait()

time: 56.4 us -> 56.4 us (level)
  no operation moved by 1% of the time
where the time goes in v3:
time: 56.4 us; the launch traced here: 56.3 us
  Pallas kernels  55.6 us (99%)
  between operations  0.64 us (1%)
    pallas_call x1, Pallas kernels, on_device(): pl.pallas_call(lambda *refs: kernel(n_space, n_tm, *refs), out_shape=(jax...  54 us
    pallas_call x1, Pallas kernels, on_device(): pl.pallas_call(hand_on, out_shape=(jax.ShapeDtypeStruct((384, 128), F32),...  1.62 us

profile of v3, /device:TPU:8, one launch (start us, length us, event | category | flops | bytes accessed | tf_op | source)
XLA Modules:
  0.0 56.3 jit_solution(2690619122687018455)
XLA Ops:
  0.6 54.0 %shard_map.86 = (f32[384,128]{1,0:T(8,128)}, f32[2,8,24]{2,1,0:T(8,128)}) custom-call(f32[384,128]{1,0:T(8,128)} %bitcast.49, f32[384,128]{1,0:T(8,128)} %bitcast.50, bf16[1152,128]{1,0:T(8,128)(2,1)} %bitcast.47, bf16[2304,128]{1,0:T(8,128)(2,1)} %bitcast.46, s32[4,128]{1,0:T(4,128)} %bitcast.51, bf16[9216,128]{1,0:T(8,128)(2,1)} %bitcast.45, ...), custom_call_target="tpu_custom_call" | custom-call | tf_op jit(solution)/shard_map/pallas_call | solution.py:593
  54.6 1.6 %shard_map.87 = (f32[384,128]{1,0:T(8,128)}, f32[2,8,24]{2,1,0:T(8,128)}) custom-call(f32[384,128]{1,0:T(8,128)} %get-tuple-element.6.smooth_in, f32[2,8,24]{2,1,0:T(8,128)} %get-tuple-element.7.coarse_in), custom_call_target="tpu_custom_call" | custom-call | tf_op jit(solution)/shard_map/pallas_call | solution.py:645
